TPU v7x, 32 devices: a whole 2x2x4 slice. The times are simulated.
32 devices in a mesh: gz: 16 (over z, y, core), row: 2 (over x).
Axes of the slice: x: 2, y: 2, z: 4, core: 2. Of those that a mesh axis runs over, the one named last changes fastest.
Arguments:
- axial_vel: float32 [1024, 256, 256], P('gz', 'row'), may hold values from -6 to 6
- radial_vel: float32 [1024, 256, 256], P('gz', 'row'), may hold values from -6 to 6
- swirl_vel: float32 [1024, 256, 256], P('gz', 'row'), may hold values from -6 to 6
- inflow_rate: float32 [48], replicated, may hold values from 0.25 to 2
- canopy_gore: int32 [1024, 256, 256], P('gz', 'row'), may hold values from 0 to 48, as said below
Outputs:
- axial_out: float32 [1024, 256, 256], P('gz', 'row')
- radial_projected_velocity: float32 [1024, 256, 256], P('gz', 'row')
- swirl_out: float32 [1024, 256, 256], P('gz', 'row')
Inputs may be any that keep to these rules, and one draw needn't show every extreme that they name: `canopy_gore`: a canopy cell in azimuthal column t holds gore floor(t * 48 / 256); other cells hold 48.
All inputs are finite; a program needn't handle non-finite values.
Results may differ from a plain program's by a relative error of at most 0.0009.
Values sent between devices are 32-bit elements; how exact they have to be, the bound alone decides.
A program may use at most 128 MiB of HBM per device.

v0:
```python
import math

import jax
import jax.numpy as jnp
from jax import lax
from jax.sharding import PartitionSpec as P

NX = 1024
NR = 256
NT = 256
GORES = 48


helmholtz_shift = 0.001
maximal_precision = lax.Precision.HIGHEST


def extended(block, sides, width):
    for axis, dim in sides:
        count = lax.axis_size(axis)
        forward = [(i, i + 1) for i in range(count - 1)]
        backward = [(target, source) for source, target in forward]
        low = lax.ppermute(
            lax.slice_in_dim(block, block.shape[dim] - width, None, axis=dim), axis, forward
        )
        high = lax.ppermute(lax.slice_in_dim(block, 0, width, axis=dim), axis, backward)
        block = jnp.concatenate([low, block, high], axis=dim)
    return block


def azimuth_basis(extent, mode_ids):
    positions = jnp.arange(extent, dtype=jnp.int32)
    half_way = extent // 2
    frequency = jnp.where(mode_ids <= half_way, mode_ids, mode_ids - half_way)
    phases = positions[:, None] * frequency[None, :] % extent
    angles = phases.astype(jnp.float32) * (2.0 * math.pi / extent)
    weights = jnp.where(
        (mode_ids == 0) | (mode_ids == half_way), math.sqrt(1.0 / extent), math.sqrt(2.0 / extent)
    ).astype(jnp.float32)
    return (
        jnp.where((mode_ids > half_way)[None, :], jnp.sin(angles), jnp.cos(angles))
        * weights[None, :]
    )


def azimuth_eigen(mode_ids):
    half_way = NT // 2
    frequency = jnp.where(mode_ids <= half_way, mode_ids, mode_ids - half_way)
    angles = frequency.astype(jnp.float32) * (2.0 * math.pi / NT)
    arc_step = 0.75 * NR * 2.0 * math.pi / NT
    return (2.0 - 2.0 * jnp.cos(angles)) / (arc_step * arc_step)


def axial_basis(extent):
    indices = jnp.arange(extent, dtype=jnp.int32) + 1
    phases = indices[:, None] * indices[None, :] % (2 * (extent + 1))
    angles = phases.astype(jnp.float32) * (math.pi / (extent + 1))
    return jnp.sin(angles) * math.sqrt(2.0 / (extent + 1))


def axial_eigen(extent):
    indices = jnp.arange(extent, dtype=jnp.int32) + 1
    return 2.0 - 2.0 * jnp.cos(indices.astype(jnp.float32) * (math.pi / (extent + 1)))


def radial_basis(extent):
    mode_ids = jnp.arange(extent, dtype=jnp.int32)[:, None]
    cell_ids = jnp.arange(extent, dtype=jnp.int32)[None, :]
    phases = mode_ids * (2 * cell_ids + 1) % (4 * extent)
    angles = phases.astype(jnp.float32) * (math.pi / (2 * extent))
    weights = jnp.where(mode_ids == 0, math.sqrt(1.0 / extent), math.sqrt(2.0 / extent)).astype(
        jnp.float32
    )
    return jnp.cos(angles) * weights


def radial_eigen(mode_ids):
    return 2.0 - 2.0 * jnp.cos(mode_ids.astype(jnp.float32) * (math.pi / NR))


def cell_radius(cell_ids):
    return cell_ids.astype(jnp.float32) + (0.25 * NR + 0.5)


def denominator_of(mode_ids, radial_ids):
    total = azimuth_eigen(mode_ids)[:, None, None] + axial_eigen(NX)[None, :, None]
    return total + radial_eigen(radial_ids)[None, None, :] + helmholtz_shift


def canopy_source(gore_map, rate_table):
    gore_ids = jnp.arange(rate_table.shape[0], dtype=jnp.int32)
    column_gore = jnp.arange(NT, dtype=jnp.int32) * GORES // NT
    matches = column_gore[:, None] == gore_ids[None, :]
    column_rate = jnp.sum(jnp.where(matches, rate_table[None, :], 0.0), axis=1)
    return jnp.where(gore_map < GORES, column_rate[None, None, :], 0.0)


def body(axial_vel, radial_vel, swirl_vel, inflow_rate, canopy_gore):
    radial_block = axial_vel.shape[1]
    row_index = lax.axis_index("row")
    gz_index = lax.axis_index("gz")
    row_count = lax.axis_size("row")
    spacing = 2.0 * math.pi / NT
    own_first = row_index * radial_block
    own_cells = own_first + jnp.arange(radial_block, dtype=jnp.int32)
    radius = cell_radius(own_cells)[None, :, None]
    axial_pad = extended(axial_vel, (("gz", 0),), 1)
    radial_flux = extended(radial_vel * radius, (("row", 1),), 1)
    divergence = 0.5 * (axial_pad[2:] - axial_pad[:-2])
    divergence = divergence + (radial_flux[:, 2:] - radial_flux[:, :-2]) / (2.0 * radius)
    divergence = divergence + (jnp.roll(swirl_vel, -1, 2) - jnp.roll(swirl_vel, 1, 2)) / (
        2.0 * radius * spacing
    )
    right_side = divergence - canopy_source(canopy_gore, inflow_rate)
    all_modes = jnp.arange(NT, dtype=jnp.int32)
    spectrum_in = jnp.einsum(
        "xrt,tm->mxr", right_side, azimuth_basis(NT, all_modes), precision=maximal_precision
    )
    axial_lookup_table = axial_basis(NX)
    radial_table = radial_basis(NR)
    resident_modes = lax.all_to_all(spectrum_in, "gz", split_axis=0, concat_axis=1, tiled=True)
    modes_each = resident_modes.shape[0]
    mode_ids = gz_index * modes_each + jnp.arange(modes_each, dtype=jnp.int32)
    axial_coefficient = jnp.einsum(
        "wo,aoy->awy", axial_lookup_table, resident_modes, precision=maximal_precision
    )
    mine_rows = lax.dynamic_slice_in_dim(radial_table, own_first, radial_block, 0)
    mine_cols = lax.dynamic_slice_in_dim(radial_table, own_first, radial_block, 1)
    spectrum = jnp.einsum(
        "sj,mkj->mks",
        mine_rows,
        lax.all_gather(axial_coefficient, "row", axis=2, tiled=True),
        precision=maximal_precision,
    )
    scaled = spectrum / denominator_of(mode_ids, own_cells)
    radial_returned = jnp.einsum(
        "sj,mks->mkj",
        mine_cols,
        lax.all_gather(scaled, "row", axis=2, tiled=True),
        precision=maximal_precision,
    )
    physical_space = jnp.einsum(
        "ov,hox->hvx", axial_lookup_table, radial_returned, precision=maximal_precision
    )
    returned = lax.all_to_all(physical_space, "gz", split_axis=1, concat_axis=0, tiled=True)
    pressure = -jnp.einsum(
        "qxr,tq->xrt", returned, azimuth_basis(NT, all_modes), precision=maximal_precision
    )
    padded = extended(pressure, (("gz", 0), ("row", 1)), 1)
    lower_ghost = jnp.where(row_index == 0, pressure[:, :1], padded[1:-1, :1])
    upper_ghost = jnp.where(row_index == row_count - 1, pressure[:, -1:], padded[1:-1, -1:])
    above = jnp.concatenate([pressure[:, 1:], upper_ghost], axis=1)
    below = jnp.concatenate([lower_ghost, pressure[:, :-1]], axis=1)
    axial_out = axial_vel - 0.5 * (padded[2:, 1:-1] - padded[:-2, 1:-1])
    radial_projected_velocity = radial_vel - 0.5 * (above - below)
    swirl_out = swirl_vel - (jnp.roll(pressure, -1, 2) - jnp.roll(pressure, 1, 2)) / (
        2.0 * radius * spacing
    )
    return (axial_out, radial_projected_velocity, swirl_out)


def solution(mesh):
    placed = (
        P("gz", "row", None),
        P("gz", "row", None),
        P("gz", "row", None),
        P(),
        P("gz", "row", None),
    )
    return jax.shard_map(
        body,
        mesh=mesh,
        in_specs=placed,
        out_specs=(P("gz", "row", None), P("gz", "row", None), P("gz", "row", None)),
        check_vma=False,
    )
```

profile of v0, /device:TPU:13, one launch (start us, length us, event | category | flops | bytes accessed | tf_op | source)
XLA Modules:
  0.0 1109.6 jit_solution(17983961640131257172)
XLA Ops:
  7.2 0.0 slice-start
  7.2 0.0 slice-start.1
  7.2 4.4 broadcast_multiply_fusion
  11.6 0.0 copy-start
  11.6 0.1 fusion.115
  11.7 1.6 collective-permute-start.2
  13.3 4.0 collective-permute-start.3
  17.3 1.0 fusion.114
  18.3 3.1 collective-permute-start
  21.4 3.3 collective-permute-start.1
  24.7 0.0 slice-done
  24.8 0.0 slice-done.1
  24.8 7.5 fusion.113
  32.2 0.0 copy-done
  32.3 4.9 fusion.112
  37.1 0.1 select_reduce_fusion
  37.2 0.0 collective-permute-done.2
  37.3 0.0 collective-permute-done.3
  37.3 0.0 collective-permute-done
  37.3 0.0 collective-permute-done.1
  37.3 34.2 %fusion.17 = f32[256,64,128]{2,0,1:T(8,128)} fusion(f32[64,128,256]{2,1,0:T(8,128)} %copy-done, f32[64,1,256]{2,1,0:T(1,128)S(1)} %collective-permute-done.3, f32[64,1,256]{2,1,0:T(1,128)S(1)} %collective-permute-done.2, f32[64,128,256]{2,1,0:T(8,128)} %param.5, f32[1,128,256]{2,1,0:T(8,128)S(1)} %collective-permute-done.1, ...), kind=kOutput, calls=%fused_computation.27 | convolution fusion | flops 6479151104 | bytes 50729216 | tf_op jit(solution)/shard_map/xrt,tm->mxr/dot_general | solution.py:116
  71.5 11.6 %copy.35 = f32[256,64,128]{2,1,0:T(8,128)} copy(f32[256,64,128]{2,0,1:T(8,128)} %fusion.17) | data formatting | bytes 16777216 | tf_op jit(solution)/shard_map/xrt,tm->mxr/dot_general | solution.py:116
  83.2 5.0 all-to-all-start
  88.2 0.0 all-gather.3.cloned.1.call-start
  88.2 17.4 %fusion.126 = f32[1024,1024,1]{1,0,2:T(8,128)} fusion(s32[1024]{0:T(1024)S(1)} %iota_add_fusion), kind=kLoop, calls=%fused_computation.33.clone.1.clone.clone.clone.1 | loop fusion | flops 10485760 | bytes 4198400 | tf_op jit(solution)/shard_map/wo,aoy->awy/dot_general | solution.py:124
  105.6 164.9 %all-to-all-done = f32[256,64,128]{2,1,0:T(8,128)} async-done(((f32[256,64,128]{2,1,0:T(8,128)}), f32[256,64,128]{2,1,0:T(8,128)}, u32[]{:S(2)}, u32[]{:S(2)}) %all-to-all-start) | async-done | bytes 8388640 | tf_op jit(solution)/shard_map/all_to_all | solution.py:121
  270.5 4.4 copy.36
  274.9 0.2 copy-done.2
  275.1 56.0 %fusion.40 = f32[16,1024,128]{1,2,0:T(8,128)} fusion(f32[16,1024,128]{2,1,0:T(8,128)S(1)} %bitcast.53, f32[1024,1024,1]{1,0,2:T(8,128)S(1)} %copy-done.2), kind=kOutput, calls=%fused_computation.48 | convolution fusion | flops 25769803776 | bytes 20971520 | tf_op jit(solution)/shard_map/wo,aoy->awy/dot_general | solution.py:124
  331.0 0.0 all-gather.3.cloned.1.call-update
  331.1 0.0 all-gather.5.cloned.1.call-start
  331.2 0.1 fusion.85
  331.3 0.1 broadcast_add_fusion
  331.4 1.0 fusion.65
  332.3 196.3 %all-gather.3.cloned.1.call-done = f32[16,1024,256]{1,2,0:T(8,128)} async-done(((f32[16,1024,128]{1,2,0:T(8,128)}), f32[16,1024,256]{1,2,0:T(8,128)}) %all-gather.3.cloned.1.call-update) | async-done | bytes 16777232 | tf_op jit(solution)/shard_map/all_gather | solution.py:132
  528.6 34.3 %add_divide_fusion = f32[16,1024,128]{2,1,0:T(8,128)} fusion(f32[128]{0:T(128)S(1)} %multiply_subtract_fusion.1, f32[16,1024]{1,0:T(8,128)S(1)} %broadcast_add_fusion, f32[16,1024,256]{1,2,0:T(8,128)} %all-gather.3.cloned.1.call-done, f32[256,256]{1,0:T(8,128)S(1)} %fusion.65, s32[]{:T(128)S(6)} %select_n.117), kind=kOutput, calls=%fused_computation.26 | convolution fusion | flops 6448742400 | bytes 25362948 | tf_op jit(solution)/shard_map/sj,mkj->mks/dot_general | solution.py:129
  563.0 0.0 all-gather.5.cloned.1.call-update
  563.0 17.4 %fusion.128 = f32[1024,1024,1]{1,0,2:T(8,128)} fusion(s32[1024]{0:T(1024)S(1)} %iota_add_fusion), kind=kLoop, calls=%fused_computation.33.clone.clone.clone.clone.1 | loop fusion | flops 10485760 | bytes 4198400 | tf_op jit(solution)/shard_map/ov,hox->hvx/dot_general | solution.py:142
  580.4 181.6 %all-gather.5.cloned.1.call-done = f32[16,1024,256]{2,1,0:T(8,128)} async-done(((f32[16,1024,128]{2,1,0:T(8,128)}), f32[16,1024,256]{2,1,0:T(8,128)}) %all-gather.5.cloned.1.call-update) | async-done | bytes 16777232 | tf_op jit(solution)/shard_map/all_gather | solution.py:139
  762.0 22.9 %fusion.74 = f32[16,1024,128]{1,2,0:T(8,128)S(1)} fusion(f32[16,1024,256]{2,1,0:T(8,128)} %all-gather.5.cloned.1.call-done, f32[256,256]{1,0:T(8,128)S(1)} %fusion.65, s32[]{:T(128)S(6)} %select_n.117), kind=kOutput, calls=%fused_computation.85 | convolution fusion | flops 6442450944 | bytes 25296900 | tf_op jit(solution)/shard_map/sj,mks->mkj/dot_general | solution.py:136
  784.9 30.5 %fusion.43 = f32[16,1024,128]{1,2,0:T(8,128)} fusion(f32[16,1024,128]{1,2,0:T(8,128)S(1)} %fusion.74, f32[1024,1024,1]{1,0,2:T(8,128)S(1)} %copy-done.1), kind=kOutput, calls=%fused_computation.49 | convolution fusion | flops 25769803776 | bytes 20971520 | tf_op jit(solution)/shard_map/ov,hox->hvx/dot_general | solution.py:142
  815.4 9.1 copy.40
  824.5 6.5 all-to-all-start.1
  831.1 182.2 %all-to-all-done.1 = f32[16,1024,128]{2,0,1:T(8,128)} async-done(((f32[16,1024,128]{2,0,1:T(8,128)}), f32[16,1024,128]{2,0,1:T(8,128)}, u32[]{:S(2)}, u32[]{:S(2)}) %all-to-all-start.1) | async-done | bytes 8388640 | tf_op jit(solution)/shard_map/all_to_all | solution.py:145
  1013.3 6.0 copy.42
  1019.2 18.9 %fusion.37 = f32[64,128,256]{2,1,0:T(8,128)S(1)} fusion(f32[256,64,128]{2,1,0:T(8,128)S(1)} %bitcast.52, f32[256]{0:T(256)S(1)} %or_select_fusion, s32[256]{0:T(256)S(1)} %compare_select_fusion, pred[256]{0:T(512)(128)(4,1)S(1)} %iota_compare_fusion.2), kind=kOutput, calls=%fused_computation.47 | convolution fusion | flops 6445596672 | bytes 16779520 | tf_op jit(solution)/shard_map/qxr,tq->xrt/dot_general | solution.py:146
  1038.1 7.5 fusion.109
  1045.6 4.9 fusion.108
  1050.5 2.1 collective-permute-start.4
  1052.6 4.3 collective-permute-start.5
  1057.0 16.5 %fusion.14 = f32[64,128,256]{2,1,0:T(8,128)} fusion(f32[64,128,256]{2,1,0:T(8,128)} %param.7, f32[64,128,1]{2,1,0:T(8,128)} %get-tuple-element.6, f32[64,128,255]{2,1,0:T(8,128)} %get-tuple-element.8, f32[64,128,255]{2,1,0:T(8,128)} %get-tuple-element.7, f32[64,128,1]{2,1,0:T(8,128)} %get-tuple-element.5, f32[128]{0:T(128)S(1)} %get-tuple-element.23), kind=kLoop, calls=%fused_computation.23 | loop fusion | flops 10485760 | bytes 33554944 | tf_op jit(solution)/shard_map/sub | solution.py:156
  1073.5 6.6 fusion.110
  1080.1 0.0 collective-permute-done.4
  1080.1 0.0 collective-permute-done.5
  1080.1 0.1 pad_maximum_fusion.6
  1080.2 1.3 collective-permute-start.6
  1081.5 0.0 slice-start.2
  1081.5 0.0 slice-start.3
  1081.5 4.3 collective-permute-start.7
  1085.8 7.0 fusion.2
  1092.7 0.0 collective-permute-done.6
  1092.7 0.0 collective-permute-done.7
  1092.7 0.2 broadcast_select_fusion
  1092.9 9.4 fusion.12
  (21 shorter events, 0.2 us)
Async XLA Ops:
  7.2 17.6 %slice-start = ((s8[8388608]{0:T(1024)(128)(4,1)}), s8[4194304]{0:T(1024)(128)(4,1)S(1)}, s32[]{:S(2)}) async-start(s8[8388608]{0:T(1024)(128)(4,1)} %bitcast.48), calls=%async_computation.4 | async-start | bytes 8388608
  7.2 17.6 %slice-start.1 = ((s8[8388608]{0:T(1024)(128)(4,1)}), s8[4194304]{0:T(1024)(128)(4,1)S(1)}, s32[]{:S(2)}) async-start(s8[8388608]{0:T(1024)(128)(4,1)} %bitcast.48), calls=%async_computation.5 | async-start | bytes 8388608
  11.6 20.7 %copy-start = (f32[64,128,256]{2,1,0:T(8,128)}, f32[64,128,256]{2,1,0:T(8,128)S(1)}, u32[]{:S(2)}) copy-start(f32[64,128,256]{2,1,0:T(8,128)S(1)} %broadcast_multiply_fusion) | copy-start | bytes 25165828
  11.7 25.5 %collective-permute-start.2 = (f32[64,1,256]{2,1,0:T(1,128)S(1)}, f32[64,1,256]{2,1,0:T(1,128)S(1)}, u32[]{:S(2)}, u32[]{:S(2)}) collective-permute-start(f32[64,1,256]{2,1,0:T(1,128)S(1)} %get-tuple-element.21), channel_id=1, source_target_pairs={{1,0},{3,2},{5,4},{7,6},{9,8},{11,10},{13,12},{15,14},{17,16},{19,... | collective-permute-start | bytes 196616 | tf_op jit(solution)/shard_map/ppermute | solution.py:26
  13.3 24.0 %collective-permute-start.3 = (f32[64,1,256]{2,1,0:T(1,128)S(1)}, f32[64,1,256]{2,1,0:T(1,128)S(1)}, u32[]{:S(2)}, u32[]{:S(2)}) collective-permute-start(f32[64,1,256]{2,1,0:T(1,128)S(1)} %get-tuple-element.22), channel_id=1, source_target_pairs={{0,1},{2,3},{4,5},{6,7},{8,9},{10,11},{12,13},{14,15},{16,17},{18,... | collective-permute-start | bytes 196616 | tf_op jit(solution)/shard_map/ppermute | solution.py:23
  18.3 19.0 %collective-permute-start = (f32[1,128,256]{2,1,0:T(8,128)S(1)}, f32[1,128,256]{2,1,0:T(8,128)S(1)}, u32[]{:S(2)}, u32[]{:S(2)}) collective-permute-start(f32[1,128,256]{2,1,0:T(8,128)S(1)} %get-tuple-element.19), channel_id=1, source_target_pairs={{2,0},{4,2},{6,4},{8,6},{10,8},{12,10},{14,12},{16,14},{18,16},{20... | collective-permute-start | bytes 393224 | tf_op jit(solution)/shard_map/ppermute | solution.py:26
  21.4 15.9 %collective-permute-start.1 = (f32[1,128,256]{2,1,0:T(8,128)S(1)}, f32[1,128,256]{2,1,0:T(8,128)S(1)}, u32[]{:S(2)}, u32[]{:S(2)}) collective-permute-start(f32[1,128,256]{2,1,0:T(8,128)S(1)} %get-tuple-element.20), channel_id=1, source_target_pairs={{0,2},{2,4},{4,6},{6,8},{8,10},{10,12},{12,14},{14,16},{16,18},{18... | collective-permute-start | bytes 393224 | tf_op jit(solution)/shard_map/ppermute | solution.py:23
  32.3 4.9 copy-start.3
  83.2 187.3 %all-to-all-start = ((f32[256,64,128]{2,1,0:T(8,128)}), f32[256,64,128]{2,1,0:T(8,128)}, u32[]{:S(2)}, u32[]{:S(2)}) async-start(f32[256,64,128]{2,1,0:T(8,128)} %copy.35), calls=%async_computation | async-start | bytes 16777216 | tf_op jit(solution)/shard_map/all_to_all | solution.py:121
  88.2 440.5 %all-gather.3.cloned.1.call-start = ((), (), s32[]{:S(2)}) async-start(), calls=%async_computation.2 | async-start | bytes 25165824 | tf_op jit(solution)/shard_map/all_gather | solution.py:132
  270.5 4.6 copy-start.2
  331.1 430.9 %all-gather.5.cloned.1.call-start = ((), (), s32[]{:S(2)}) async-start(), calls=%async_computation.3 | async-start | bytes 25165824 | tf_op jit(solution)/shard_map/all_gather | solution.py:139
  762.0 22.9 %copy-start.1 = (f32[1024,1024,1]{1,0,2:T(8,128)S(1)}, f32[1024,1024,1]{1,0,2:T(8,128)}, u32[]{:S(2)}) copy-start(f32[1024,1024,1]{1,0,2:T(8,128)} %fusion.128) | copy-start | bytes 12582916
  824.5 188.7 %all-to-all-start.1 = ((f32[16,1024,128]{2,0,1:T(8,128)}), f32[16,1024,128]{2,0,1:T(8,128)}, u32[]{:S(2)}, u32[]{:S(2)}) async-start(f32[16,1024,128]{2,0,1:T(8,128)} %copy.40), calls=%async_computation.1 | async-start | bytes 16777216 | tf_op jit(solution)/shard_map/all_to_all | solution.py:145
  1050.5 29.6 %collective-permute-start.4 = (f32[1,128,256]{2,1,0:T(8,128)S(1)}, f32[1,128,256]{2,1,0:T(8,128)S(1)}, u32[]{:S(2)}, u32[]{:S(2)}) collective-permute-start(f32[1,128,256]{2,1,0:T(8,128)S(1)} %get-tuple-element.13), channel_id=1, source_target_pairs={{2,0},{4,2},{6,4},{8,6},{10,8},{12,10},{14,12},{16,14},{18,16},{20... | collective-permute-start | bytes 393224 | tf_op jit(solution)/shard_map/ppermute | solution.py:26
  1052.6 27.5 %collective-permute-start.5 = (f32[1,128,256]{2,1,0:T(8,128)S(1)}, f32[1,128,256]{2,1,0:T(8,128)S(1)}, u32[]{:S(2)}, u32[]{:S(2)}) collective-permute-start(f32[1,128,256]{2,1,0:T(8,128)S(1)} %get-tuple-element.14), channel_id=1, source_target_pairs={{0,2},{2,4},{4,6},{6,8},{8,10},{10,12},{12,14},{14,16},{16,18},{18... | collective-permute-start | bytes 393224 | tf_op jit(solution)/shard_map/ppermute | solution.py:23
  1080.2 12.5 %collective-permute-start.6 = (f32[66,1,256]{2,1,0:T(1,128)S(1)}, f32[66,1,256]{2,1,0:T(1,128)S(1)}, u32[]{:S(2)}, u32[]{:S(2)}) collective-permute-start(f32[66,1,256]{2,1,0:T(1,128)S(1)} %get-tuple-element.4), channel_id=1, source_target_pairs={{1,0},{3,2},{5,4},{7,6},{9,8},{11,10},{13,12},{15,14},{17,16},{19,... | collective-permute-start | bytes 202760 | tf_op jit(solution)/shard_map/ppermute | solution.py:26
  1081.5 11.4 %slice-start.2 = ((s8[8388608]{0:T(1024)(128)(4,1)}), s8[4194304]{0:T(1024)(128)(4,1)S(1)}, s32[]{:S(2)}) async-start(s8[8388608]{0:T(1024)(128)(4,1)} %bitcast.50), calls=%async_computation.6 | async-start | bytes 8388608
  1081.5 11.4 %slice-start.3 = ((s8[8388608]{0:T(1024)(128)(4,1)}), s8[4194304]{0:T(1024)(128)(4,1)S(1)}, s32[]{:S(2)}) async-start(s8[8388608]{0:T(1024)(128)(4,1)} %bitcast.50), calls=%async_computation.7 | async-start | bytes 8388608
  1081.5 11.2 %collective-permute-start.7 = (f32[66,1,256]{2,1,0:T(1,128)S(1)}, f32[66,1,256]{2,1,0:T(1,128)S(1)}, u32[]{:S(2)}, u32[]{:S(2)}) collective-permute-start(f32[66,1,256]{2,1,0:T(1,128)S(1)} %get-tuple-element.3), channel_id=1, source_target_pairs={{0,1},{2,3},{4,5},{6,7},{8,9},{10,11},{12,13},{14,15},{16,17},{18,... | collective-permute-start | bytes 202760 | tf_op jit(solution)/shard_map/ppermute | solution.py:23
Sparse Core Ops, SparseCore 0:
  331.2 197.3 all-gather.2
  563.1 198.8 all-gather.4
where the time goes:
time: 1120 us; the launch traced here: 1110 us
  waiting for transfers between devices  725 us (65%)
  matrix products  197 us (18%)
  other arithmetic  73.7 us (7%)
  local copies, waits for them, and re-layouts  63.7 us (6%)
  starting transfers between devices  35.6 us (3%)
  between operations  14.8 us (1%)
    all_gather x1, waiting for transfers between devices, body(): lax.all_gather(axial_coefficient, 'row', axis=2, tiled=True)  196 us
    all_to_all x1, waiting for transfers between devices, body(): lax.all_to_all(physical_space, 'gz', split_axis=1, concat_axis=0, tiled=T...  182 us
    all_gather x1, waiting for transfers between devices, body(): lax.all_gather(scaled, 'row', axis=2, tiled=True)  182 us
    all_to_all x1, waiting for transfers between devices, body(): lax.all_to_all(spectrum_in, 'gz', split_axis=0, concat_axis=1, tiled=True)  165 us
    dot_general x1, matrix products, body(): jnp.einsum('wo,aoy->awy', axial_lookup_table, resident_modes, precision=m...  56 us
    dot_general x1, matrix products, body(): jnp.einsum('sj,mkj->mks', mine_rows, lax.all_gather(axial_coefficient, 'r...  34.3 us
    dot_general x1, matrix products, body(): jnp.einsum('xrt,tm->mxr', right_side, azimuth_basis(NT, all_modes), preci...  34.2 us
    dot_general x1, matrix products, body(): jnp.einsum('ov,hox->hvx', axial_lookup_table, radial_returned, precision=...  30.5 us
  transfers between devices with their start and end apart: 12, of which 4 were waited for; matrix products, arithmetic and copies ran while one was open for 7% of the time, Pallas kernels for 0%

commit v1 on v0

v1 whole, which is shorter than its diff:
```python
import functools
import math

import jax
import jax.numpy as jnp
import ml_dtypes
import numpy as np
from jax import lax
from jax.experimental import pallas as pl
from jax.experimental.pallas import tpu as pltpu
from jax.sharding import PartitionSpec as P


SHIFT = 0.001
GORES = 48
XB = 8
F32 = jnp.float32
BF16 = jnp.bfloat16
NN = (((1,), (0,)), ((), ()))
NT_ = (((1,), (1,)), ((), ()))
MIB = 1024 * 1024


def np_split(table):
    high = table.astype(np.float32).astype(ml_dtypes.bfloat16)
    low = (table - high.astype(np.float64)).astype(np.float32).astype(ml_dtypes.bfloat16)
    return high, low


@functools.lru_cache(maxsize=None)
def tables(nx, nr, nt, x_each):
    half = nr // 2
    modes = np.arange(nt)
    freq = np.where(modes <= nt // 2, modes, modes - nt // 2)
    angle = 2 * np.pi * ((np.arange(nt)[None, :] * freq[:, None]) % nt) / nt
    weight = np.where((modes == 0) | (modes == nt // 2), math.sqrt(1 / nt), math.sqrt(2 / nt))
    azimuth = np.where((modes > nt // 2)[:, None], np.sin(angle), np.cos(angle)) * weight[:, None]
    arc = 0.75 * nr * 2 * np.pi / nt
    az = (2 - 2 * np.cos(2 * np.pi * freq / nt)) / arc**2
    s = np.arange(half)
    v = np.where(s == 0, math.sqrt(1 / half), math.sqrt(2 / half))
    radial = np.cos(np.pi * (s[None, :] * (2 * s[:, None] + 1) % (4 * half)) / (2 * half)) * v[None]
    edge = radial[0]
    ra = 2 - 2 * np.cos(np.pi * s / half)
    lam = az[:, None] + ra[None, :] + SHIFT
    t = lam / 2
    r = 1 / (1 + t + np.sqrt(lam + t * t))
    k = np.arange(nx) + 1
    axial = math.sqrt(2 / (nx + 1)) * np.sin(
        np.pi * ((k[:, None] * k[None, :]) % (2 * (nx + 1))) / (nx + 1)
    )
    ax = 2 - 2 * np.cos(np.pi * k / (nx + 1))
    couple = np.zeros((nt, nx))
    for m in range(nt):
        couple[m] = (2 * edge[:, None] ** 2 / (ax[None, :] + lam[m][:, None])).sum(0)
    jump = 1 / (1 + couple)
    power = r**x_each
    kappa = r * (1 - power**2) / (1 - r * r)
    total = r * (1 - r ** (2 * nx)) / (1 - r * r)
    image = r / (1 + r * total)
    thin = np.stack([power, kappa, image], axis=1)
    return dict(
        azimuth=np_split(azimuth),
        radial=np_split(radial),
        radial_flip=np_split(radial[::-1].copy()),
        axial=np_split(axial),
        edge=edge.astype(np.float32)[None],
        r=r.astype(np.float32),
        logr=np.log(r).astype(np.float32),
        rr=(1 / (1 - r * r)).astype(np.float32),
        jump=jump.astype(np.float32),
        thin=thin.astype(np.float32),
    )


def split(x):
    high = x.astype(BF16)
    return high, (x - high.astype(F32)).astype(BF16)


def dot3(a, b, dims):
    dot = functools.partial(lax.dot_general, dimension_numbers=dims, preferred_element_type=F32)
    return dot(a[0], b[0]) + (dot(a[0], b[1]) + dot(a[1], b[0]))


def forward_kernel(
    ax, axp, axn, lo, hi, rv, sw, go, gup, gdn, rate, rad, hinv, sinv, ch, cl, sh, sl, r, e,
    y_out, send, ysc, yc,
):
    step = pl.program_id(0)
    steps = pl.num_programs(0)
    nt = ax.shape[2]
    x_each = ysc.shape[0]

    @pl.when(step == 0)
    def _():
        yc[...] = jnp.zeros_like(yc)

    first, last = step == 0, step == steps - 1
    cc = (ch[...], cl[...])
    ss = (sh[...], sl[...])
    for x in range(XB):
        before = ax[x - 1] if x > 0 else jnp.where(first, lo[0], axp[0])
        after = ax[x + 1] if x < XB - 1 else jnp.where(last, hi[0], axn[0])
        flux = rv[x] * rad[...]
        above = jnp.concatenate([flux[1:], gup[x : x + 1]], axis=0)
        below = jnp.concatenate([gdn[x : x + 1], flux[:-1]], axis=0)
        swirl = sw[x]
        right = 0.5 * (after - before) + (above - below) * hinv[...]
        right = right + (pltpu.roll(swirl, nt - 1, 1) - pltpu.roll(swirl, 1, 1)) * sinv[...]
        right = right - jnp.where(go[x] < GORES, rate[...], 0.0)
        part = dot3(cc, split(right), NT_)
        part = dot3(split(part), ss, NN)
        y = r[...] * (part + yc[...])
        yc[...] = y
        y_out[x] = y
        ysc[step * XB + x] = y

    @pl.when(last)
    def _():
        half = r.shape[1]
        send[:, :half] = yc[...]
        yc[...] = jnp.zeros_like(yc)
        send[:, 2 * half :] = jnp.zeros_like(yc)
        lane = lax.broadcasted_iota(jnp.int32, yc.shape, 1)

        def back(n, carry):
            i = x_each - 1 - n
            p = ysc[i] + r[...] * yc[...]
            yc[...] = p
            g = jnp.sum(p * e[...], axis=1, keepdims=True)
            send[:, 2 * half :] = jnp.where(lane == i, g, send[:, 2 * half :])
            return carry

        lax.fori_loop(0, x_each, back, 0)
        send[:, half : 2 * half] = yc[...]


def thin_kernel(recv, coef, const, e, jump, xh, xl, out, left, gsc, hsc, esc):
    blocks, _, own, _ = recv.shape
    half = e.shape[1]
    x_each = coef.shape[1]
    power, kappa, image = const[:, 0], const[:, 1], const[:, 2]

    def scan(forward, backward):
        def run(start):
            inlet = [start]
            for b in range(blocks - 1):
                inlet.append(forward(b) + power * inlet[-1])
            outlet = [None] * blocks
            outlet[-1] = jnp.zeros_like(start)
            for b in range(blocks - 1, -1, -1):
                value = backward(b) + inlet[b] * kappa + power * outlet[b]
                if b:
                    outlet[b - 1] = value
            return inlet, outlet, value

        value = run(jnp.zeros_like(power))[2]
        return run(-image * value)[:2]

    for row in range(2):
        inlet, outlet = scan(
            lambda b: recv[b, row, :, :half], lambda b: recv[b, row, :, half : 2 * half]
        )
        for b in range(blocks):
            out[b, row, :, :half] = inlet[b]
            out[b, row, :, half : 2 * half] = outlet[b]
    for b in range(blocks):
        left[b, :, :half] = (out[b, 0, :, :half] - out[b, 1, :, :half]) * e[...]
        left[b, :, half:] = (
            out[b, 0, :, half : 2 * half] - out[b, 1, :, half : 2 * half]
        ) * e[...]
    for m in range(own):
        value = dot3(split(left[:, m, :]), split(coef[m]), NT_)
        gsc[:, m, :] = value
    total = None
    for b in range(blocks):
        g = gsc[b] + (
            recv[b, 0, :, 2 * half : 2 * half + x_each]
            - recv[b, 1, :, 2 * half : 2 * half + x_each]
        )
        rows = slice(b * x_each, (b + 1) * x_each)
        term = dot3(split(g), (xh[rows, :], xl[rows, :]), NN)
        total = term if total is None else total + term
    h = dot3(split(total * jump[...]), (xh[...], xl[...]), NN)
    for b in range(blocks):
        hsc[b] = h[:, b * x_each : (b + 1) * x_each]
    for m in range(own):
        value = dot3(split(hsc[:, m, :]), split(coef[m]), NN)
        esc[:, m, :] = value
    inlet, outlet = scan(lambda b: esc[b, :, half:] * e[...], lambda b: esc[b, :, :half] * e[...])
    for b in range(blocks):
        for row, sign in ((0, -1.0), (1, 1.0)):
            out[b, row, :, :half] += sign * inlet[b]
            out[b, row, :, half : 2 * half] += sign * outlet[b]
            out[b, row, :, 2 * half :] = jnp.zeros((own, half), F32)
            out[b, row, :, 2 * half : 2 * half + x_each] = hsc[b]


def backward_kernel(
    y_hbm, recv, ax, rv, sw, dup, ddn, hsw, ch, cl, sh, sl, r, e,
    ax_out, rv_out, sw_out, ysc, pressure, pc, sem,
):
    step = pl.program_id(0)
    steps = pl.num_programs(0)
    half = r.shape[1]
    nt = ax.shape[2]
    x_each = ysc.shape[0] - 1
    cc = (ch[...], cl[...])
    ss = (sh[...], sl[...])

    def inverse(p):
        return dot3(split(dot3(ss, split(p), NT_)), cc, NN)

    def fetch(c):
        return pltpu.make_async_copy(
            y_hbm.at[pl.ds(c * XB, XB)], ysc.at[pl.ds(1 + c * XB, XB)], sem.at[c]
        )

    @pl.when(step == 0)
    def _():
        for c in range(x_each // XB):
            fetch(c).start()
        ysc[0] = recv[:, :half]
        pc[...] = recv[:, :half]
        lane = lax.broadcasted_iota(jnp.int32, pc.shape, 1)
        for c in range(x_each // XB):
            fetch(c).wait()

            def ahead(n, carry):
                i = c * XB + n
                h = jnp.sum(
                    jnp.where(lane == i, recv[:, 2 * half :], 0.0), axis=1, keepdims=True
                )
                z = r[...] * (pc[...] + h * e[...])
                pc[...] = z
                ysc[1 + i] += z
                return carry

            lax.fori_loop(0, XB, ahead, 0)
        outlet = recv[:, half : 2 * half]
        pressure[XB + 1] = inverse(outlet)
        p = ysc[x_each] + r[...] * outlet
        pc[...] = p
        pressure[XB] = inverse(p)

    @pl.when(step > 0)
    def _():
        pressure[XB] = pressure[0]
        pressure[XB + 1] = pressure[1]

    block = steps - 1 - step
    for d in range(XB):
        p = ysc[block * XB + XB - 1 - d] + r[...] * pc[...]
        pc[...] = p
        pressure[XB - 1 - d] = inverse(p)
    for x in range(XB):
        here = pressure[x + 1]
        ax_out[x] = ax[x] + 0.5 * (pressure[x + 2] - pressure[x])
        above = jnp.concatenate([here[1:], here[-1:] + dup[x : x + 1]], axis=0)
        below = jnp.concatenate([here[:1] + ddn[x : x + 1], here[:-1]], axis=0)
        rv_out[x] = rv[x] + 0.5 * (above - below)
        sw_out[x] = sw[x] + (pltpu.roll(here, nt - 1, 1) - pltpu.roll(here, 1, 1)) * hsw[...]


def body(axial_vel, radial_vel, swirl_vel, inflow_rate, canopy_gore):
    x_each, half, nt = axial_vel.shape
    blocks = lax.axis_size("gz")
    rows = lax.axis_size("row")
    assert rows == 2
    nx, nr = x_each * blocks, half * rows
    count = blocks * rows
    own = nt // count
    tab = tables(nx, nr, nt, x_each)
    row = lax.axis_index("row")
    me = lax.axis_index("gz") * rows + row
    top = row == 0
    spacing = 2.0 * math.pi / nt
    ids = row * half + jnp.arange(half, dtype=jnp.int32)
    radius = jnp.broadcast_to((ids.astype(F32) + (0.25 * nr + 0.5))[:, None], (half, nt))
    hinv = 0.5 / radius
    sinv = 0.5 / (radius * spacing)
    up = [(i, i + 1) for i in range(blocks - 1)]
    down = [(i + 1, i) for i in range(blocks - 1)]
    lo = lax.ppermute(axial_vel[-1:], "gz", up)
    hi = lax.ppermute(axial_vel[:1], "gz", down)
    edge = jnp.where(top, radial_vel[:, half - 1], radial_vel[:, 0])
    ghost = lax.ppermute(edge, "row", [(0, 1), (1, 0)])
    gup = jnp.where(top, ghost * (0.25 * nr + 0.5 + half), 0.0)
    gdn = jnp.where(top, 0.0, ghost * (0.25 * nr - 0.5 + half))
    column = np.arange(nt) * GORES // nt
    hot = (column[:, None] == np.arange(GORES)[None, :]).astype(np.float32)
    rate = jnp.sum(jnp.where(hot > 0, inflow_rate[None, :], 0.0), axis=1)[None, :]
    ch, cl = (jnp.asarray(a) for a in tab["azimuth"])
    sh, sl = (jnp.where(top, a, b) for a, b in zip(tab["radial_flip"], tab["radial"]))
    r = jnp.asarray(tab["r"])
    e = jnp.asarray(tab["edge"])
    steps = x_each // XB
    width = 3 * half

    def whole(*shape):
        return pl.BlockSpec(shape, lambda i: (0,) * len(shape))

    block = pl.BlockSpec((XB, half, nt), lambda i: (i, 0, 0))
    line = pl.BlockSpec((XB, nt), lambda i: (i, 0))
    y, send = pl.pallas_call(
        forward_kernel,
        grid=(steps,),
        in_specs=[
            block,
            pl.BlockSpec((1, half, nt), lambda i: (jnp.maximum(i * XB - 1, 0), 0, 0)),
            pl.BlockSpec((1, half, nt), lambda i: (jnp.minimum(i * XB + XB, x_each - 1), 0, 0)),
            whole(1, half, nt), whole(1, half, nt),
            block, block, block, line, line,
            whole(1, nt), whole(half, nt), whole(half, nt), whole(half, nt),
            whole(nt, nt), whole(nt, nt), whole(half, half), whole(half, half),
            whole(nt, half), whole(1, half),
        ],
        out_specs=[pl.BlockSpec((XB, nt, half), lambda i: (i, 0, 0)), whole(nt, width)],
        out_shape=[
            jax.ShapeDtypeStruct((x_each, nt, half), F32),
            jax.ShapeDtypeStruct((nt, width), F32),
        ],
        scratch_shapes=[pltpu.VMEM((x_each, nt, half), F32), pltpu.VMEM((nt, half), F32)],
        compiler_params=pltpu.CompilerParams(vmem_limit_bytes=48 * MIB),
        name="forward",
    )(
        axial_vel, axial_vel, axial_vel, lo, hi, radial_vel, swirl_vel, canopy_gore, gup, gdn,
        rate, radius, hinv, sinv, ch, cl, sh, sl, r, e,
    )

    recv = lax.all_to_all(send, ("gz", "row"), split_axis=0, concat_axis=0, tiled=True)
    recv = recv.reshape(blocks, rows, own, width)

    def mine(table):
        return lax.dynamic_slice_in_dim(jnp.asarray(table), me * own, own, 0)

    place = jnp.arange(x_each, dtype=F32)[None, :, None]
    logr = mine(tab["logr"])[:, None, :]
    near = jnp.exp(logr * (place + 1)) * (1 - jnp.exp(logr * (2 * x_each - 2 * place)))
    coef = jnp.concatenate(
        [near * mine(tab["rr"])[:, None, :], jnp.exp(logr * (x_each - place))], axis=2
    )
    vm = pl.BlockSpec(memory_space=pltpu.VMEM)
    answer = pl.pallas_call(
        thin_kernel,
        in_specs=[vm] * 7,
        out_specs=vm,
        out_shape=jax.ShapeDtypeStruct((blocks, rows, own, width), F32),
        scratch_shapes=[
            pltpu.VMEM((blocks, own, 2 * half), F32),
            pltpu.VMEM((blocks, own, x_each), F32),
            pltpu.VMEM((blocks, own, x_each), F32),
            pltpu.VMEM((blocks, own, 2 * half), F32),
        ],
        compiler_params=pltpu.CompilerParams(vmem_limit_bytes=48 * MIB),
        name="thin",
    )(recv, coef, mine(tab["thin"]), e, mine(tab["jump"]), *(jnp.asarray(a) for a in tab["axial"]))

    back = lax.all_to_all(
        answer.reshape(nt, width), ("gz", "row"), split_axis=0, concat_axis=0, tiled=True
    )
    jump = jnp.einsum(
        "mi,mt->it",
        back[:, 2 * half : 2 * half + x_each],
        ch.astype(F32) + cl.astype(F32),
        precision=lax.Precision.HIGHEST,
    )
    dup = jnp.where(top, -jump, 0.0)
    ddn = jnp.where(top, 0.0, jump)
    block = pl.BlockSpec((XB, half, nt), lambda i: (steps - 1 - i, 0, 0))
    line = pl.BlockSpec((XB, nt), lambda i: (steps - 1 - i, 0))
    shape = jax.ShapeDtypeStruct(axial_vel.shape, F32)
    return pl.pallas_call(
        backward_kernel,
        grid=(steps,),
        in_specs=[
            pl.BlockSpec(memory_space=pl.ANY), whole(nt, width), block, block, block, line, line,
            whole(half, nt), whole(nt, nt), whole(nt, nt), whole(half, half), whole(half, half),
            whole(nt, half), whole(1, half),
        ],
        out_specs=[block, block, block],
        out_shape=[shape, shape, shape],
        scratch_shapes=[
            pltpu.VMEM((x_each + 1, nt, half), F32),
            pltpu.VMEM((XB + 2, half, nt), F32),
            pltpu.VMEM((nt, half), F32),
            pltpu.SemaphoreType.DMA((steps,)),
        ],
        compiler_params=pltpu.CompilerParams(vmem_limit_bytes=48 * MIB),
        name="backward",
    )(
        y, back, axial_vel, radial_vel, swirl_vel, dup, ddn, sinv, ch, cl, sh, sl, r,
        jnp.where(top, -e, e),
    )


def solution(mesh):
    placed = P("gz", "row", None)
    return jax.shard_map(
        body,
        mesh=mesh,
        in_specs=(placed, placed, placed, P(), placed),
        out_specs=(placed, placed, placed),
        check_vma=False,
    )
```

time: 1120 us -> 131 us (0.12)
  the two profiles are of different devices: /device:TPU:13 before, /device:TPU:1 now
where the time goes in v1:
time: 131 us; the launch traced here: 130 us
  Pallas kernels  72.4 us (55%)
  waiting for transfers between devices  23 us (18%)
  starting transfers between devices  17 us (13%)
  local copies, waits for them, and re-layouts  13.2 us (10%)
  other arithmetic  2.54 us (2%)
  matrix products  1.32 us (1%)
    pallas_call x1, Pallas kernels, body(): pl.pallas_call(forward_kernel, grid=(steps,), in_specs=[block, pl.BlockSp...  37.2 us
    pallas_call x1, Pallas kernels, body(): pl.pallas_call(backward_kernel, grid=(steps,), in_specs=[pl.BlockSpec(mem...  31.4 us
    all_to_all x1, waiting for transfers between devices, body(): lax.all_to_all(answer.reshape(nt, width), ('gz', 'row'), split_axis=0, co...  12.5 us
    all_to_all x1, waiting for transfers between devices, body(): lax.all_to_all(send, ('gz', 'row'), split_axis=0, concat_axis=0, tiled=True)  10.1 us
    unnamed x30, local copies, waits for them, and re-layouts  7.91 us
    all_to_all x1, starting transfers between devices, body(): lax.all_to_all(send, ('gz', 'row'), split_axis=0, concat_axis=0, tiled=True)  6.41 us
    pallas_call x1, Pallas kernels, body(): pl.pallas_call(thin_kernel, in_specs=[vm] * 7, out_specs=vm, out_shape=ja...  3.77 us
    ppermute x1, starting transfers between devices, body(): lo = lax.ppermute(axial_vel[-1:], 'gz', up)  3.05 us
  transfers between devices with their start and end apart: 5, of which 3 were waited for; matrix products, arithmetic and copies ran while one was open for 5% of the time, Pallas kernels for 0%

profile of v1, /device:TPU:1, one launch (start us, length us, event | category | flops | bytes accessed | tf_op | source)
XLA Modules:
  0.0 130.4 jit_solution(3443113432491119725)
XLA Ops:
  0.6 1.3 fusion.3
  2.0 2.1 %collective-permute-start.2 = (f32[64,256]{1,0:T(8,128)S(1)}, f32[64,256]{1,0:T(8,128)S(1)}, u32[]{:S(2)}, u32[]{:S(2)}) collective-permute-start(f32[64,256]{1,0:T(8,128)S(1)} %fusion.2), channel_id=1, source_target_pairs={{0,1},{1,0},{2,3},{3,2},{4,5},{5,4},{6,7},{7,6},{8,9},{9,8},{10,11... | collective-permute-start | bytes 196616 | tf_op jit(solution)/shard_map/ppermute | solution.py:288
  4.1 1.0 fusion.4
  5.1 2.9 %collective-permute-start.1 = (f32[1,128,256]{2,1,0:T(8,128)S(1)}, f32[1,128,256]{2,1,0:T(8,128)S(1)}, u32[]{:S(2)}, u32[]{:S(2)}) collective-permute-start(f32[1,128,256]{2,1,0:T(8,128)S(1)} %get-tuple-element.9), channel_id=1, source_target_pairs={{2,0},{4,2},{6,4},{8,6},{10,8},{12,10},{14,12},{16,14},{18,16},{20... | collective-permute-start | bytes 393224 | tf_op jit(solution)/shard_map/ppermute | solution.py:286
  7.9 3.0 %collective-permute-start = (f32[1,128,256]{2,1,0:T(8,128)S(1)}, f32[1,128,256]{2,1,0:T(8,128)S(1)}, u32[]{:S(2)}, u32[]{:S(2)}) collective-permute-start(f32[1,128,256]{2,1,0:T(8,128)S(1)} %get-tuple-element.10), channel_id=1, source_target_pairs={{0,2},{2,4},{4,6},{6,8},{8,10},{10,12},{12,14},{14,16},{16,18},{18... | collective-permute-start | bytes 393224 | tf_op jit(solution)/shard_map/ppermute | solution.py:285
  11.0 0.8 select_reduce_fusion
  11.8 0.8 broadcast_select_fusion.1
  12.6 0.0 copy-start.8
  12.6 0.0 copy-start.10
  12.7 0.0 collective-permute-done.2
  12.7 0.0 collective-permute-done.1.hi
  12.7 0.3 collective-permute-done.lo
  13.0 0.1 broadcast_in_dim.43.sinv.hsw
  13.1 0.1 broadcast_in_dim.42.hinv
  13.2 0.1 broadcast_in_dim.41.rad
  13.2 0.0 copy-start.2
  13.2 0.9 copy-done.2
  14.1 0.0 copy-start.4
  14.1 0.9 copy-done.4
  15.0 0.0 copy-start.6
  15.1 0.9 copy-done.6
  16.0 0.0 copy-start.13
  16.0 0.7 copy-done.13
  16.6 0.0 copy-start
  16.6 37.2 %forward.1 = (f32[64,256,128]{2,1,0:T(8,128)}, f32[256,384]{1,0:T(8,128)}) custom-call(f32[64,128,256]{2,1,0:T(8,128)} %ax.3, f32[64,128,256]{2,1,0:T(8,128)} %ax.3, f32[64,128,256]{2,1,0:T(8,128)} %ax.3, f32[1,128,256]{2,1,0:T(8,128)S(1)} %collective-permute-done.lo, f32[1,128,256]{2,1,0:T(8,128)S(1)} %collective-permute-done.1.hi, f32[64,128,256]{2,1,0:T(8,128)} %rv.3, ...), custom_call_target="tpu_custom_call" | custom-call | tf_op jit(solution)/shard_map/forward/pallas_call | solution.py:306
  53.8 0.0 copy-done.8
  53.8 0.0 copy-done.10
  53.8 0.0 copy-start.3
  53.8 0.0 copy-start.5
  53.8 0.0 copy-start.7
  53.8 6.4 %all-to-all-start = ((f32[32,8,384]{2,1,0:T(8,128)}), f32[32,8,384]{2,1,0:T(8,128)S(1)}, u32[]{:S(2)}, u32[]{:S(2)}) async-start(f32[32,8,384]{2,1,0:T(8,128)} %bitcast.2), calls=%async_computation | async-start | bytes 786432 | tf_op jit(solution)/shard_map/all_to_all | solution.py:332
  60.3 0.7 constant_dynamic-slice_fusion.2
  61.0 0.7 constant_dynamic-slice_fusion.1.const
  61.7 1.4 %constant_dynamic-slice_fusion.jump = f32[8,1024]{1,0:T(8,128)} fusion(f32[256,1024]{1,0:T(8,128)} %constant.81.clone, s32[]{:T(128)S(6)} %select_n.73), kind=kLoop, calls=%fused_computation.14 | loop fusion | bytes 65540 | tf_op jit(solution)/shard_map/dynamic_slice | solution.py:336
  63.1 0.2 multiply_multiply_fusion
  63.3 10.1 %all-to-all-done = f32[32,8,384]{2,1,0:T(8,128)S(1)} async-done(((f32[32,8,384]{2,1,0:T(8,128)}), f32[32,8,384]{2,1,0:T(8,128)S(1)}, u32[]{:S(2)}, u32[]{:S(2)}) %all-to-all-start) | async-done | bytes 393248 | tf_op jit(solution)/shard_map/all_to_all | solution.py:332
  73.5 0.0 copy-done
  73.5 0.0 copy-start.1
  73.5 1.6 %copy-done.1 = bf16[1024,1024]{1,0:T(8,128)(2,1)S(1)} copy-done((bf16[1024,1024]{1,0:T(8,128)(2,1)S(1)}, bf16[1024,1024]{1,0:T(8,128)(2,1)}, u32[]{:S(2)}) %copy-start.1) | copy-done | bytes 2097176
  75.1 0.0 copy-start.12
  75.1 0.8 copy-done.12
  75.8 0.0 copy-start.14
  75.8 0.7 copy-done.14
  76.5 3.8 %thin.1 = f32[16,2,8,384]{3,2,1,0:T(8,128)} custom-call(f32[16,2,8,384]{3,2,1,0:T(8,128)S(1)} %bitcast.10, f32[8,64,256]{2,1,0:T(8,128)S(1)} %pad_maximum_fusion.coef, f32[8,3,128]{2,1,0:T(4,128)S(1)} %constant_dynamic-slice_fusion.1.const, f32[1,128]{1,0:T(1,128)S(1)} %copy-done.14, f32[8,1024]{1,0:T(8,128)S(1)} %copy-done.12, ...), custom_call_target="tpu_custom_call" | custom-call | tf_op jit(solution)/shard_map/thin/pallas_call | solution.py:345
  80.2 2.6 %all-to-all-start.1 = ((f32[32,8,384]{2,1,0:T(8,128)}), f32[32,8,384]{2,1,0:T(8,128)S(1)}, u32[]{:S(2)}, u32[]{:S(2)}) async-start(f32[32,8,384]{2,1,0:T(8,128)} %bitcast.4), calls=%async_computation.1 | async-start | bytes 786432 | tf_op jit(solution)/shard_map/all_to_all | solution.py:360
  82.9 0.7 broadcast_select_fusion.3.e
  83.5 12.5 %all-to-all-done.1 = f32[32,8,384]{2,1,0:T(8,128)S(1)} async-done(((f32[32,8,384]{2,1,0:T(8,128)}), f32[32,8,384]{2,1,0:T(8,128)S(1)}, u32[]{:S(2)}, u32[]{:S(2)}) %all-to-all-start.1) | async-done | bytes 393248 | tf_op jit(solution)/shard_map/all_to_all | solution.py:360
  96.1 1.3 %broadcast_select_fusion = (f32[64,256]{1,0:T(8,128)S(1)}, f32[64,256]{1,0:T(8,128)S(1)}) fusion(pred[]{:T(512)S(6)} %eq.3, f32[256,256]{1,0:T(8,128)} %constant.86, f32[256,384]{1,0:T(8,128)S(1)} %bitcast.8), kind=kOutput, calls=%fused_computation.11 | convolution fusion | flops 50380800 | bytes 524289 | tf_op jit(solution)/shard_map/mi,mt->it/dot_general | solution.py:363
  97.4 0.0 copy-done.3
  97.4 0.0 copy-done.5
  97.4 0.0 copy-done.7
  97.4 0.0 copy-start.9
  97.4 0.7 copy-done.9
  98.2 0.0 copy-start.11
  98.2 0.8 copy-done.11
  98.9 31.4 %backward.1 = (f32[64,128,256]{2,1,0:T(8,128)}, f32[64,128,256]{2,1,0:T(8,128)}, f32[64,128,256]{2,1,0:T(8,128)}) custom-call(f32[64,256,128]{2,1,0:T(8,128)} %get-tuple-element.5.y_hbm, f32[256,384]{1,0:T(8,128)S(1)} %bitcast.9, f32[64,128,256]{2,1,0:T(8,128)} %ax.3, f32[64,128,256]{2,1,0:T(8,128)} %rv.3, f32[64,128,256]{2,1,0:T(8,128)} %sw.3, ...), custom_call_target="tpu_custom_call" | custom-call | tf_op jit(solution)/shard_map/backward/pallas_call | solution.py:374
  (7 shorter events, 0.1 us)
Async XLA Ops:
  2.0 10.7 %collective-permute-start.2 = (f32[64,256]{1,0:T(8,128)S(1)}, f32[64,256]{1,0:T(8,128)S(1)}, u32[]{:S(2)}, u32[]{:S(2)}) collective-permute-start(f32[64,256]{1,0:T(8,128)S(1)} %fusion.2), channel_id=1, source_target_pairs={{0,1},{1,0},{2,3},{3,2},{4,5},{5,4},{6,7},{7,6},{8,9},{9,8},{10,11... | collective-permute-start | bytes 196616 | tf_op jit(solution)/shard_map/ppermute | solution.py:288
  5.1 7.6 %collective-permute-start.1 = (f32[1,128,256]{2,1,0:T(8,128)S(1)}, f32[1,128,256]{2,1,0:T(8,128)S(1)}, u32[]{:S(2)}, u32[]{:S(2)}) collective-permute-start(f32[1,128,256]{2,1,0:T(8,128)S(1)} %get-tuple-element.9), channel_id=1, source_target_pairs={{2,0},{4,2},{6,4},{8,6},{10,8},{12,10},{14,12},{16,14},{18,16},{20... | collective-permute-start | bytes 393224 | tf_op jit(solution)/shard_map/ppermute | solution.py:286
  7.9 5.1 %collective-permute-start = (f32[1,128,256]{2,1,0:T(8,128)S(1)}, f32[1,128,256]{2,1,0:T(8,128)S(1)}, u32[]{:S(2)}, u32[]{:S(2)}) collective-permute-start(f32[1,128,256]{2,1,0:T(8,128)S(1)} %get-tuple-element.10), channel_id=1, source_target_pairs={{0,2},{2,4},{4,6},{6,8},{8,10},{10,12},{12,14},{14,16},{16,18},{18... | collective-permute-start | bytes 393224 | tf_op jit(solution)/shard_map/ppermute | solution.py:285
  12.6 41.2 %copy-start.8 = (bf16[128,128]{1,0:T(8,128)(2,1)}, bf16[128,128]{1,0:T(8,128)(2,1)S(1)}, u32[]{:S(2)}) copy-start(bf16[128,128]{1,0:T(8,128)(2,1)S(1)} %get-tuple-element.17.sl) | copy-start | bytes 98308
  12.6 41.2 %copy-start.10 = (bf16[128,128]{1,0:T(8,128)(2,1)}, bf16[128,128]{1,0:T(8,128)(2,1)S(1)}, u32[]{:S(2)}) copy-start(bf16[128,128]{1,0:T(8,128)(2,1)S(1)} %get-tuple-element.18.sh) | copy-start | bytes 98308
  13.2 0.9 copy-start.2
  14.1 0.9 copy-start.4
  15.0 0.9 copy-start.6
  16.0 0.7 copy-start.13
  16.6 56.8 %copy-start = (bf16[1024,1024]{1,0:T(8,128)(2,1)S(1)}, bf16[1024,1024]{1,0:T(8,128)(2,1)}, u32[]{:S(2)}) copy-start(bf16[1024,1024]{1,0:T(8,128)(2,1)} %constant.83.clone.xl) | copy-start | bytes 6291460
  53.8 43.6 %copy-start.3 = (f32[256,128]{1,0:T(8,128)S(1)}, f32[256,128]{1,0:T(8,128)}, u32[]{:S(2)}) copy-start(f32[256,128]{1,0:T(8,128)} %constant.76.clone.r) | copy-start | bytes 393220
  53.8 43.6 %copy-start.5 = (bf16[256,256]{1,0:T(8,128)(2,1)S(1)}, bf16[256,256]{1,0:T(8,128)(2,1)}, u32[]{:S(2)}) copy-start(bf16[256,256]{1,0:T(8,128)(2,1)} %constant.71.clone.cl) | copy-start | bytes 393220
  53.8 43.6 %copy-start.7 = (bf16[256,256]{1,0:T(8,128)(2,1)S(1)}, bf16[256,256]{1,0:T(8,128)(2,1)}, u32[]{:S(2)}) copy-start(bf16[256,256]{1,0:T(8,128)(2,1)} %constant.70.clone.ch) | copy-start | bytes 393220
  53.8 19.6 %all-to-all-start = ((f32[32,8,384]{2,1,0:T(8,128)}), f32[32,8,384]{2,1,0:T(8,128)S(1)}, u32[]{:S(2)}, u32[]{:S(2)}) async-start(f32[32,8,384]{2,1,0:T(8,128)} %bitcast.2), calls=%async_computation | async-start | bytes 786432 | tf_op jit(solution)/shard_map/all_to_all | solution.py:332
  73.5 1.6 %copy-start.1 = (bf16[1024,1024]{1,0:T(8,128)(2,1)S(1)}, bf16[1024,1024]{1,0:T(8,128)(2,1)}, u32[]{:S(2)}) copy-start(bf16[1024,1024]{1,0:T(8,128)(2,1)} %constant.82.clone.xh) | copy-start | bytes 6291460
  75.1 0.8 copy-start.12
  75.8 0.7 copy-start.14
  80.2 15.8 %all-to-all-start.1 = ((f32[32,8,384]{2,1,0:T(8,128)}), f32[32,8,384]{2,1,0:T(8,128)S(1)}, u32[]{:S(2)}, u32[]{:S(2)}) async-start(f32[32,8,384]{2,1,0:T(8,128)} %bitcast.4), calls=%async_computation.1 | async-start | bytes 786432 | tf_op jit(solution)/shard_map/all_to_all | solution.py:360
  97.4 0.8 copy-start.9
  98.2 0.8 copy-start.11

commit v2 on v1

--- a/solution.py
+++ b/solution.py
@@ -61,6 +61,7 @@
     thin = np.stack([power, kappa, image], axis=1)
     return dict(
         azimuth=np_split(azimuth),
+        flat=(azimuth * radial[0, 0]).astype(np.float32),
         radial=np_split(radial),
         radial_flip=np_split(radial[::-1].copy()),
         axial=np_split(axial),
@@ -198,7 +199,7 @@
 
 
 def backward_kernel(
-    y_hbm, recv, ax, rv, sw, dup, ddn, hsw, ch, cl, sh, sl, r, e,
+    y_hbm, recv, ax, rv, sw, dup, ddn, hsw, ch, cl, cf, sh, sl, r, e,
     ax_out, rv_out, sw_out, ysc, pressure, pc, sem,
 ):
     step = pl.program_id(0)
@@ -210,7 +211,9 @@
     ss = (sh[...], sl[...])
 
     def inverse(p):
-        return dot3(split(dot3(ss, split(p), NT_)), cc, NN)
+        flat = jnp.sum(p[:, :1] * cf[...], axis=0, keepdims=True)
+        rest = jnp.where(lax.broadcasted_iota(jnp.int32, p.shape, 1) == 0, 0.0, p)
+        return dot3(split(dot3(ss, split(rest), NT_)), cc, NN) + flat
 
     def fetch(c):
         return pltpu.make_async_copy(
@@ -376,8 +379,8 @@
         grid=(steps,),
         in_specs=[
             pl.BlockSpec(memory_space=pl.ANY), whole(nt, width), block, block, block, line, line,
-            whole(half, nt), whole(nt, nt), whole(nt, nt), whole(half, half), whole(half, half),
-            whole(nt, half), whole(1, half),
+            whole(half, nt), whole(nt, nt), whole(nt, nt), whole(nt, nt), whole(half, half),
+            whole(half, half), whole(nt, half), whole(1, half),
         ],
         out_specs=[block, block, block],
         out_shape=[shape, shape, shape],
@@ -390,7 +393,7 @@
         compiler_params=pltpu.CompilerParams(vmem_limit_bytes=48 * MIB),
         name="backward",
     )(
-        y, back, axial_vel, radial_vel, swirl_vel, dup, ddn, sinv, ch, cl, sh, sl, r,
+        y, back, axial_vel, radial_vel, swirl_vel, dup, ddn, sinv, ch, cl, jnp.asarray(tab["flat"]), sh, sl, r,
         jnp.where(top, -e, e),
     )
 

time: 131 us -> 132 us (level)
    unnamed x30 -> x32, local copies, waits for them, and re-layouts: 7.91 us -> 8.86 us
where the time goes in v2:
time: 132 us
  Pallas kernels  72.6 us (55%)
  waiting for transfers between devices  23 us (17%)
  starting transfers between devices  17 us (13%)
  local copies, waits for them, and re-layouts  14.2 us (11%)
  other arithmetic  2.54 us (2%)
  matrix products  1.32 us (1%)
    pallas_call x1, Pallas kernels, body(): pl.pallas_call(forward_kernel, grid=(steps,), in_specs=[block, pl.BlockSp...  37.2 us
    pallas_call x1, Pallas kernels, body(): pl.pallas_call(backward_kernel, grid=(steps,), in_specs=[pl.BlockSpec(mem...  31.6 us
    all_to_all x1, waiting for transfers between devices, body(): lax.all_to_all(answer.reshape(nt, width), ('gz', 'row'), split_axis=0, co...  12.5 us
    all_to_all x1, waiting for transfers between devices, body(): lax.all_to_all(send, ('gz', 'row'), split_axis=0, concat_axis=0, tiled=True)  10.1 us
    unnamed x32, local copies, waits for them, and re-layouts  8.86 us
    all_to_all x1, starting transfers between devices, body(): lax.all_to_all(send, ('gz', 'row'), split_axis=0, concat_axis=0, tiled=True)  6.41 us
    pallas_call x1, Pallas kernels, body(): pl.pallas_call(thin_kernel, in_specs=[vm] * 7, out_specs=vm, out_shape=ja...  3.77 us
    ppermute x1, starting transfers between devices, body(): lo = lax.ppermute(axial_vel[-1:], 'gz', up)  3.05 us
  transfers between devices with their start and end apart: 5, of which 3 were waited for; matrix products, arithmetic and copies ran while one was open for 5% of the time, Pallas kernels for 0%

profile of v2, /device:TPU:1, one launch (start us, length us, event | category | flops | bytes accessed | tf_op | source)
XLA Modules:
  0.0 131.5 jit_solution(1442613561726414713)
XLA Ops:
  0.6 1.3 fusion.3
  2.0 2.1 %collective-permute-start.2 = (f32[64,256]{1,0:T(8,128)S(1)}, f32[64,256]{1,0:T(8,128)S(1)}, u32[]{:S(2)}, u32[]{:S(2)}) collective-permute-start(f32[64,256]{1,0:T(8,128)S(1)} %fusion.2), channel_id=1, source_target_pairs={{0,1},{1,0},{2,3},{3,2},{4,5},{5,4},{6,7},{7,6},{8,9},{9,8},{10,11... | collective-permute-start | bytes 196616 | tf_op jit(solution)/shard_map/ppermute | solution.py:291
  4.1 1.0 fusion.4
  5.1 2.9 %collective-permute-start.1 = (f32[1,128,256]{2,1,0:T(8,128)S(1)}, f32[1,128,256]{2,1,0:T(8,128)S(1)}, u32[]{:S(2)}, u32[]{:S(2)}) collective-permute-start(f32[1,128,256]{2,1,0:T(8,128)S(1)} %get-tuple-element.9), channel_id=1, source_target_pairs={{2,0},{4,2},{6,4},{8,6},{10,8},{12,10},{14,12},{16,14},{18,16},{20... | collective-permute-start | bytes 393224 | tf_op jit(solution)/shard_map/ppermute | solution.py:289
  7.9 3.0 %collective-permute-start = (f32[1,128,256]{2,1,0:T(8,128)S(1)}, f32[1,128,256]{2,1,0:T(8,128)S(1)}, u32[]{:S(2)}, u32[]{:S(2)}) collective-permute-start(f32[1,128,256]{2,1,0:T(8,128)S(1)} %get-tuple-element.10), channel_id=1, source_target_pairs={{0,2},{2,4},{4,6},{6,8},{8,10},{10,12},{12,14},{14,16},{16,18},{18... | collective-permute-start | bytes 393224 | tf_op jit(solution)/shard_map/ppermute | solution.py:288
  11.0 0.8 select_reduce_fusion
  11.8 0.8 broadcast_select_fusion.1
  12.6 0.0 copy-start.8
  12.6 0.0 copy-start.10
  12.7 0.0 collective-permute-done.2
  12.7 0.0 collective-permute-done.1.hi
  12.7 0.3 collective-permute-done.lo
  13.0 0.1 broadcast_in_dim.43.sinv.hsw
  13.1 0.1 broadcast_in_dim.42.hinv
  13.2 0.1 broadcast_in_dim.41.rad
  13.2 0.0 copy-start.2
  13.2 0.9 copy-done.2
  14.1 0.0 copy-start.4
  14.1 0.9 copy-done.4
  15.0 0.0 copy-start.6
  15.1 0.9 copy-done.6
  16.0 0.0 copy-start.14
  16.0 0.7 copy-done.14
  16.6 0.0 copy-start
  16.6 37.2 %forward.1 = (f32[64,256,128]{2,1,0:T(8,128)}, f32[256,384]{1,0:T(8,128)}) custom-call(f32[64,128,256]{2,1,0:T(8,128)} %ax.3, f32[64,128,256]{2,1,0:T(8,128)} %ax.3, f32[64,128,256]{2,1,0:T(8,128)} %ax.3, f32[1,128,256]{2,1,0:T(8,128)S(1)} %collective-permute-done.lo, f32[1,128,256]{2,1,0:T(8,128)S(1)} %collective-permute-done.1.hi, f32[64,128,256]{2,1,0:T(8,128)} %rv.3, ...), custom_call_target="tpu_custom_call" | custom-call | tf_op jit(solution)/shard_map/forward/pallas_call | solution.py:309
  53.8 0.0 copy-done.8
  53.8 0.0 copy-done.10
  53.8 0.0 copy-start.3
  53.8 0.0 copy-start.5
  53.8 0.0 copy-start.7
  53.8 6.4 %all-to-all-start = ((f32[32,8,384]{2,1,0:T(8,128)}), f32[32,8,384]{2,1,0:T(8,128)S(1)}, u32[]{:S(2)}, u32[]{:S(2)}) async-start(f32[32,8,384]{2,1,0:T(8,128)} %bitcast.2), calls=%async_computation | async-start | bytes 786432 | tf_op jit(solution)/shard_map/all_to_all | solution.py:335
  60.3 0.7 constant_dynamic-slice_fusion.2
  61.0 0.7 constant_dynamic-slice_fusion.1.const
  61.7 1.4 %constant_dynamic-slice_fusion.jump = f32[8,1024]{1,0:T(8,128)} fusion(f32[256,1024]{1,0:T(8,128)} %constant.83.clone, s32[]{:T(128)S(6)} %select_n.73), kind=kLoop, calls=%fused_computation.14 | loop fusion | bytes 65540 | tf_op jit(solution)/shard_map/dynamic_slice | solution.py:339
  63.1 0.2 multiply_multiply_fusion
  63.3 10.1 %all-to-all-done = f32[32,8,384]{2,1,0:T(8,128)S(1)} async-done(((f32[32,8,384]{2,1,0:T(8,128)}), f32[32,8,384]{2,1,0:T(8,128)S(1)}, u32[]{:S(2)}, u32[]{:S(2)}) %all-to-all-start) | async-done | bytes 393248 | tf_op jit(solution)/shard_map/all_to_all | solution.py:335
  73.5 0.0 copy-done
  73.5 0.0 copy-start.1
  73.5 1.6 %copy-done.1 = bf16[1024,1024]{1,0:T(8,128)(2,1)S(1)} copy-done((bf16[1024,1024]{1,0:T(8,128)(2,1)S(1)}, bf16[1024,1024]{1,0:T(8,128)(2,1)}, u32[]{:S(2)}) %copy-start.1) | copy-done | bytes 2097176
  75.1 0.0 copy-start.13
  75.1 0.8 copy-done.13
  75.8 0.0 copy-start.15
  75.8 0.7 copy-done.15
  76.5 3.8 %thin.1 = f32[16,2,8,384]{3,2,1,0:T(8,128)} custom-call(f32[16,2,8,384]{3,2,1,0:T(8,128)S(1)} %bitcast.10, f32[8,64,256]{2,1,0:T(8,128)S(1)} %pad_maximum_fusion.coef, f32[8,3,128]{2,1,0:T(4,128)S(1)} %constant_dynamic-slice_fusion.1.const, f32[1,128]{1,0:T(1,128)S(1)} %copy-done.15, f32[8,1024]{1,0:T(8,128)S(1)} %copy-done.13, ...), custom_call_target="tpu_custom_call" | custom-call | tf_op jit(solution)/shard_map/thin/pallas_call | solution.py:348
  80.2 2.6 %all-to-all-start.1 = ((f32[32,8,384]{2,1,0:T(8,128)}), f32[32,8,384]{2,1,0:T(8,128)S(1)}, u32[]{:S(2)}, u32[]{:S(2)}) async-start(f32[32,8,384]{2,1,0:T(8,128)} %bitcast.4), calls=%async_computation.1 | async-start | bytes 786432 | tf_op jit(solution)/shard_map/all_to_all | solution.py:363
  82.9 0.7 broadcast_select_fusion.3.e
  83.5 12.5 %all-to-all-done.1 = f32[32,8,384]{2,1,0:T(8,128)S(1)} async-done(((f32[32,8,384]{2,1,0:T(8,128)}), f32[32,8,384]{2,1,0:T(8,128)S(1)}, u32[]{:S(2)}, u32[]{:S(2)}) %all-to-all-start.1) | async-done | bytes 393248 | tf_op jit(solution)/shard_map/all_to_all | solution.py:363
  96.1 1.3 %broadcast_select_fusion = (f32[64,256]{1,0:T(8,128)S(1)}, f32[64,256]{1,0:T(8,128)S(1)}) fusion(pred[]{:T(512)S(6)} %eq.3, f32[256,256]{1,0:T(8,128)} %constant.89, f32[256,384]{1,0:T(8,128)S(1)} %bitcast.8), kind=kOutput, calls=%fused_computation.11 | convolution fusion | flops 50380800 | bytes 524289 | tf_op jit(solution)/shard_map/mi,mt->it/dot_general | solution.py:366
  97.4 0.0 copy-done.3
  97.4 0.0 copy-done.5
  97.4 0.0 copy-done.7
  97.4 0.0 copy-start.9
  97.4 0.7 copy-done.9
  98.2 0.0 copy-start.11
  98.2 0.8 copy-done.11
  98.9 0.0 copy-start.12
  98.9 0.9 copy-done.12
  99.9 31.6 %backward.1 = (f32[64,128,256]{2,1,0:T(8,128)}, f32[64,128,256]{2,1,0:T(8,128)}, f32[64,128,256]{2,1,0:T(8,128)}) custom-call(f32[64,256,128]{2,1,0:T(8,128)} %get-tuple-element.5.y_hbm, f32[256,384]{1,0:T(8,128)S(1)} %bitcast.9, f32[64,128,256]{2,1,0:T(8,128)} %ax.3, f32[64,128,256]{2,1,0:T(8,128)} %rv.3, f32[64,128,256]{2,1,0:T(8,128)} %sw.3, ...), custom_call_target="tpu_custom_call" | custom-call | tf_op jit(solution)/shard_map/backward/pallas_call | solution.py:377
  (7 shorter events, 0.1 us)
Async XLA Ops:
  2.0 10.7 %collective-permute-start.2 = (f32[64,256]{1,0:T(8,128)S(1)}, f32[64,256]{1,0:T(8,128)S(1)}, u32[]{:S(2)}, u32[]{:S(2)}) collective-permute-start(f32[64,256]{1,0:T(8,128)S(1)} %fusion.2), channel_id=1, source_target_pairs={{0,1},{1,0},{2,3},{3,2},{4,5},{5,4},{6,7},{7,6},{8,9},{9,8},{10,11... | collective-permute-start | bytes 196616 | tf_op jit(solution)/shard_map/ppermute | solution.py:291
  5.1 7.6 %collective-permute-start.1 = (f32[1,128,256]{2,1,0:T(8,128)S(1)}, f32[1,128,256]{2,1,0:T(8,128)S(1)}, u32[]{:S(2)}, u32[]{:S(2)}) collective-permute-start(f32[1,128,256]{2,1,0:T(8,128)S(1)} %get-tuple-element.9), channel_id=1, source_target_pairs={{2,0},{4,2},{6,4},{8,6},{10,8},{12,10},{14,12},{16,14},{18,16},{20... | collective-permute-start | bytes 393224 | tf_op jit(solution)/shard_map/ppermute | solution.py:289
  7.9 5.1 %collective-permute-start = (f32[1,128,256]{2,1,0:T(8,128)S(1)}, f32[1,128,256]{2,1,0:T(8,128)S(1)}, u32[]{:S(2)}, u32[]{:S(2)}) collective-permute-start(f32[1,128,256]{2,1,0:T(8,128)S(1)} %get-tuple-element.10), channel_id=1, source_target_pairs={{0,2},{2,4},{4,6},{6,8},{8,10},{10,12},{12,14},{14,16},{16,18},{18... | collective-permute-start | bytes 393224 | tf_op jit(solution)/shard_map/ppermute | solution.py:288
  12.6 41.2 %copy-start.8 = (bf16[128,128]{1,0:T(8,128)(2,1)}, bf16[128,128]{1,0:T(8,128)(2,1)S(1)}, u32[]{:S(2)}) copy-start(bf16[128,128]{1,0:T(8,128)(2,1)S(1)} %get-tuple-element.17.sl) | copy-start | bytes 98308
  12.6 41.2 %copy-start.10 = (bf16[128,128]{1,0:T(8,128)(2,1)}, bf16[128,128]{1,0:T(8,128)(2,1)S(1)}, u32[]{:S(2)}) copy-start(bf16[128,128]{1,0:T(8,128)(2,1)S(1)} %get-tuple-element.18.sh) | copy-start | bytes 98308
  13.2 0.9 copy-start.2
  14.1 0.9 copy-start.4
  15.0 0.9 copy-start.6
  16.0 0.7 copy-start.14
  16.6 56.8 %copy-start = (bf16[1024,1024]{1,0:T(8,128)(2,1)S(1)}, bf16[1024,1024]{1,0:T(8,128)(2,1)}, u32[]{:S(2)}) copy-start(bf16[1024,1024]{1,0:T(8,128)(2,1)} %constant.85.clone.xl) | copy-start | bytes 6291460
  53.8 43.6 %copy-start.3 = (f32[256,128]{1,0:T(8,128)S(1)}, f32[256,128]{1,0:T(8,128)}, u32[]{:S(2)}) copy-start(f32[256,128]{1,0:T(8,128)} %constant.78.clone.r) | copy-start | bytes 393220
  53.8 43.6 %copy-start.5 = (bf16[256,256]{1,0:T(8,128)(2,1)S(1)}, bf16[256,256]{1,0:T(8,128)(2,1)}, u32[]{:S(2)}) copy-start(bf16[256,256]{1,0:T(8,128)(2,1)} %constant.73.clone.cl) | copy-start | bytes 393220
  53.8 43.6 %copy-start.7 = (bf16[256,256]{1,0:T(8,128)(2,1)S(1)}, bf16[256,256]{1,0:T(8,128)(2,1)}, u32[]{:S(2)}) copy-start(bf16[256,256]{1,0:T(8,128)(2,1)} %constant.72.clone.ch) | copy-start | bytes 393220
  53.8 19.6 %all-to-all-start = ((f32[32,8,384]{2,1,0:T(8,128)}), f32[32,8,384]{2,1,0:T(8,128)S(1)}, u32[]{:S(2)}, u32[]{:S(2)}) async-start(f32[32,8,384]{2,1,0:T(8,128)} %bitcast.2), calls=%async_computation | async-start | bytes 786432 | tf_op jit(solution)/shard_map/all_to_all | solution.py:335
  73.5 1.6 %copy-start.1 = (bf16[1024,1024]{1,0:T(8,128)(2,1)S(1)}, bf16[1024,1024]{1,0:T(8,128)(2,1)}, u32[]{:S(2)}) copy-start(bf16[1024,1024]{1,0:T(8,128)(2,1)} %constant.84.clone.xh) | copy-start | bytes 6291460
  75.1 0.8 copy-start.13
  75.8 0.7 copy-start.15
  80.2 15.8 %all-to-all-start.1 = ((f32[32,8,384]{2,1,0:T(8,128)}), f32[32,8,384]{2,1,0:T(8,128)S(1)}, u32[]{:S(2)}, u32[]{:S(2)}) async-start(f32[32,8,384]{2,1,0:T(8,128)} %bitcast.4), calls=%async_computation.1 | async-start | bytes 786432 | tf_op jit(solution)/shard_map/all_to_all | solution.py:363
  97.4 0.8 copy-start.9
  98.2 0.8 copy-start.11
  98.9 0.9 copy-start.12
